TPU v7x, 512 devices: a whole 4x4x16 slice. The times are simulated.
512 devices in a mesh: grp: 16 (over y, x), tile: 32 (over z, core).
Axes of the slice: x: 4, y: 4, z: 16, core: 2. Of those that a mesh axis runs over, the one named last changes fastest.
Arguments:
- latent: bfloat16 [8, 64, 64, 512], P(None, 'grp', 'tile'), may hold values from -36 to 36
- coarse_filters: bfloat16 [3, 3, 3, 512, 512], P(None, None, None, None, 'grp'), may hold values from -0.0546875 to 0.0546875
- mid_filters: bfloat16 [3, 3, 3, 256, 256], P(None, None, None, None, 'tile'), may hold values from -0.078125 to 0.078125
- fine_filters: bfloat16 [3, 3, 3, 128, 128], replicated, may hold values from -0.109375 to 0.109375
- coarse_proj: bfloat16 [512, 256], replicated, may hold values from -0.25 to 0.25
- mid_proj: bfloat16 [256, 128], replicated, may hold values from -0.375 to 0.375
Outputs:
- frames_out: bfloat16 [8, 256, 256, 128], P(None, 'grp', 'tile')
All inputs are finite; a program needn't handle non-finite values.
Results may differ from a plain program's by a relative error of at most 0.018.
Values may be sent and summed in bfloat16 or wider, within the bound.
A program may use at most 128 MiB of HBM per device.

v0:
```python
import jax
import jax.numpy as jnp
from jax import lax
from jax.sharding import PartitionSpec as P


def with_halo(shard, sides, width):
    for axis, dim in sides:
        size, length = (lax.axis_size(axis), shard.shape[dim])
        up = [(i, (i + 1) % size) for i in range(size - 1)]
        down = [(j, i) for i, j in up]
        last = lax.slice_in_dim(shard, length - width, length, axis=dim)
        initial = lax.slice_in_dim(shard, 0, width, axis=dim)
        before = lax.ppermute(last, axis, up)
        after = lax.ppermute(initial, axis, down)
        shard = jnp.concatenate([before, shard, after], axis=dim)
    return shard


def activate(values):
    widened = values.astype(jnp.float32)
    scaled = widened * lax.rsqrt(jnp.mean(widened * widened, axis=-1, keepdims=True) + 1e-06)
    return jax.nn.silu(scaled).astype(jnp.bfloat16)


def double_size(values):
    return jnp.repeat(jnp.repeat(values, 2, axis=1), 2, axis=2)


def time_padded(values):
    return jnp.pad(values, ((2, 0), (0, 0), (0, 0), (0, 0)))


def stencil_columns(extended):
    padded = time_padded(extended)
    height = extended.shape[1] - 2
    breadth = extended.shape[2] - 2
    return jnp.concatenate(
        [
            padded[:, row_step : row_step + height, col_step : col_step + breadth, :]
            for row_step in range(3)
            for col_step in range(3)
        ],
        axis=-1,
    )


def apply_columns(columns, filters):
    frames = columns.shape[0] - 2
    folded = filters.reshape(3, 9 * filters.shape[3], filters.shape[4])
    total = jnp.dot(columns[0:frames], folded[0], preferred_element_type=jnp.float32)
    for frame_step in (1, 2):
        total = total + jnp.dot(
            columns[frame_step : frame_step + frames],
            folded[frame_step],
            preferred_element_type=jnp.float32,
        )
    return total


def coarse_conv(extended, filters):
    padded = time_padded(extended)
    frames = extended.shape[0]
    height = extended.shape[1] - 2
    breadth = extended.shape[2] - 2
    inputs = filters.shape[3]
    outputs = filters.shape[4]
    total = jnp.zeros((frames, height, breadth, outputs), jnp.float32)
    for frame_step in range(3):
        spread = jnp.transpose(filters[frame_step], (2, 0, 1, 3)).reshape(inputs, 9 * outputs)
        products = jnp.dot(
            padded[frame_step : frame_step + frames], spread, preferred_element_type=jnp.float32
        )
        for row_step in range(3):
            for col_step in range(3):
                lane = 3 * row_step + col_step
                total = (
                    total
                    + products[
                        :,
                        row_step : row_step + height,
                        col_step : col_step + breadth,
                        lane * outputs : (lane + 1) * outputs,
                    ]
                )
    return total


def middle_conv(extended, mid_filters):
    columns = stencil_columns(extended)
    return apply_columns(columns, lax.all_gather(mid_filters, "tile", axis=4, tiled=True))


def body(latent, coarse_filters, mid_filters, fine_filters, coarse_proj, mid_proj):
    first_act = activate(latent)
    whole = lax.all_gather(first_act, "grp", axis=1, tiled=True)
    widened = with_halo(whole, (("tile", 2),), 1)
    padded = jnp.pad(widened, ((0, 0), (1, 1), (0, 0), (0, 0)))
    filtered = coarse_conv(padded, coarse_filters).astype(jnp.bfloat16)
    returned = lax.all_to_all(filtered, "grp", split_axis=1, concat_axis=3, tiled=True)
    level_zero = (latent.astype(jnp.float32) + returned.astype(jnp.float32)).astype(jnp.bfloat16)
    reduced = jnp.dot(level_zero, coarse_proj, preferred_element_type=jnp.float32).astype(
        jnp.bfloat16
    )
    mid_act = double_size(activate(reduced))
    mid_ext = with_halo(mid_act, (("grp", 1), ("tile", 2)), 1)
    mid_terms = middle_conv(mid_ext, mid_filters)
    mid_out = (double_size(reduced).astype(jnp.float32) + mid_terms).astype(jnp.bfloat16)
    fine_low = jnp.dot(mid_out, mid_proj, preferred_element_type=jnp.float32).astype(jnp.bfloat16)
    fine_in = double_size(fine_low)
    fine_act = double_size(activate(fine_low))
    fine_ext = with_halo(fine_act, (("grp", 1), ("tile", 2)), 1)
    fine_terms = apply_columns(stencil_columns(fine_ext), fine_filters)
    return (fine_in.astype(jnp.float32) + fine_terms).astype(jnp.bfloat16)


def solution(mesh):
    in_specs = (
        P(None, "grp", "tile", None),
        P(None, None, None, None, "grp"),
        P(None, None, None, None, "tile"),
        P(),
        P(),
        P(),
    )
    out_specs = P(None, "grp", "tile", None)
    return jax.shard_map(body, mesh=mesh, in_specs=in_specs, out_specs=out_specs, check_vma=False)
```

profile of v0, /device:TPU:7, one launch (start us, length us, event | category | flops | bytes accessed | tf_op | source)
XLA Modules:
  0.0 200.4 jit_solution(11646952750403236550)
XLA Ops:
  7.6 1.6 fusion.33
  10.0 61.1 %all-gather.3.cloned.1.call-done = bf16[8,64,2,512]{3,0,2,1:T(8,128)(2,1)} async-done(((bf16[8,4,2,512]{3,0,2,1:T(8,128)(2,1)}), bf16[8,64,2,512]{3,0,2,1:T(8,128)(2,1)}) %all-gather.3.cloned.1.call-update) | async-done | bytes 1048592 | tf_op jit(solution)/shard_map/all_gather | solution.py:96
  71.1 1.8 copy.25
  73.0 5.1 %collective-permute-start = (bf16[8,64,1,512]{3,1,2,0:T(8,128)(2,1)S(1)}, bf16[8,64,1,512]{3,1,2,0:T(8,128)(2,1)S(1)}, u32[]{:S(2)}, u32[]{:S(2)}) collective-permute-start(bf16[8,64,1,512]{3,1,2,0:T(8,128)(2,1)S(1)} %get-tuple-element.8), channel_id=1, source_target_pairs={{0,1},{1,2},{2,3},{3,4},{4,5},{5,6},{6,7},{7,8},{8,9},{9,10},{10,1... | collective-permute-start | bytes 1572872 | tf_op jit(solution)/shard_map/ppermute | solution.py:14
  78.0 1.9 collective-permute-start.1
  80.0 4.1 %collective-permute-done = bf16[8,64,1,512]{3,1,2,0:T(8,128)(2,1)S(1)} collective-permute-done((bf16[8,64,1,512]{3,1,2,0:T(8,128)(2,1)S(1)}, bf16[8,64,1,512]{3,1,2,0:T(8,128)(2,1)S(1)}, u32[]{:S(2)}, u32[]{:S(2)}) %collective-permute-start) | collective-permute-done | bytes 524320 | tf_op jit(solution)/shard_map/ppermute | solution.py:14
  84.1 4.4 %collective-permute-done.1 = bf16[8,64,1,512]{3,1,2,0:T(8,128)(2,1)S(1)} collective-permute-done((bf16[8,64,1,512]{3,1,2,0:T(8,128)(2,1)S(1)}, bf16[8,64,1,512]{3,1,2,0:T(8,128)(2,1)S(1)}, u32[]{:S(2)}, u32[]{:S(2)}) %collective-permute-start.1) | collective-permute-done | bytes 524320 | tf_op jit(solution)/shard_map/ppermute | solution.py:15
  89.6 1.4 fusion.47
  91.0 1.4 fusion.50
  92.5 1.4 fusion.51
  93.9 2.5 %fusion.24 = bf16[8,64,2,32]{3,1,2,0:T(8,128)(2,1)S(1)} fusion(f32[8,66,4,288]{3,1,2,0:T(8,128)S(1)} %fusion.47, f32[8,66,4,288]{3,1,2,0:T(8,128)S(1)} %fusion.51, f32[8,66,4,288]{3,1,2,0:T(8,128)S(1)} %fusion.50), kind=kLoop, calls=%fused_computation.35 | loop fusion | flops 884736 | bytes 3604480 | tf_op jit(solution)/shard_map/convert_element_type | solution.py:99
  97.0 9.8 %all_to_all.4 = bf16[16,2,1024]{2,1,0:T(2,128)(2,1)S(1)} all-to-all(bf16[16,2,1024]{2,1,0:T(2,128)(2,1)S(1)} %reshape.91), channel_id=1, replica_groups=mesh['grp'=16,'tile'=32] {'grp'}, dimensions={0} | all-to-all | bytes 131072 | tf_op jit(solution)/shard_map/all_to_all | solution.py:100
  108.0 3.7 %collective-permute-start.2 = (bf16[8,1,4,256]{3,2,1,0:T(4,128)(2,1)S(1)}, bf16[8,1,4,256]{3,2,1,0:T(4,128)(2,1)S(1)}, u32[]{:S(2)}, u32[]{:S(2)}) collective-permute-start(bf16[8,1,4,256]{3,2,1,0:T(4,128)(2,1)S(1)} %get-tuple-element.23), channel_id=1, source_target_pairs={{0,32},{32,64},{64,96},{96,128},{128,160},{160,192},{192,224},{224... | collective-permute-start | bytes 49160 | tf_op jit(solution)/shard_map/ppermute | solution.py:14
  111.7 1.9 collective-permute-start.3
  113.7 4.6 %collective-permute-done.3 = bf16[8,1,4,256]{3,2,1,0:T(4,128)(2,1)S(1)} collective-permute-done((bf16[8,1,4,256]{3,2,1,0:T(4,128)(2,1)S(1)}, bf16[8,1,4,256]{3,2,1,0:T(4,128)(2,1)S(1)}, u32[]{:S(2)}, u32[]{:S(2)}) %collective-permute-start.3) | collective-permute-done | bytes 16416 | tf_op jit(solution)/shard_map/ppermute | solution.py:15
  118.4 4.6 %collective-permute-start.4 = (bf16[8,10,1,256]{3,2,1,0:T(2,128)(2,1)S(1)}, bf16[8,10,1,256]{3,2,1,0:T(2,128)(2,1)S(1)}, u32[]{:S(2)}, u32[]{:S(2)}) collective-permute-start(bf16[8,10,1,256]{3,2,1,0:T(2,128)(2,1)S(1)} %get-tuple-element.20), channel_id=1, source_target_pairs={{0,1},{1,2},{2,3},{3,4},{4,5},{5,6},{6,7},{7,8},{8,9},{9,10},{10,1... | collective-permute-start | bytes 122888 | tf_op jit(solution)/shard_map/ppermute | solution.py:14
  123.1 2.1 %collective-permute-start.5 = (bf16[8,10,1,256]{3,2,1,0:T(2,128)(2,1)S(1)}, bf16[8,10,1,256]{3,2,1,0:T(2,128)(2,1)S(1)}, u32[]{:S(2)}, u32[]{:S(2)}) collective-permute-start(bf16[8,10,1,256]{3,2,1,0:T(2,128)(2,1)S(1)} %get-tuple-element.21), channel_id=1, source_target_pairs={{1,0},{2,1},{3,2},{4,3},{5,4},{6,5},{7,6},{8,7},{9,8},{10,9},{11,1... | collective-permute-start | bytes 122888 | tf_op jit(solution)/shard_map/ppermute | solution.py:15
  125.6 3.7 %collective-permute-done.5 = bf16[8,10,1,256]{3,2,1,0:T(2,128)(2,1)S(1)} collective-permute-done((bf16[8,10,1,256]{3,2,1,0:T(2,128)(2,1)S(1)}, bf16[8,10,1,256]{3,2,1,0:T(2,128)(2,1)S(1)}, u32[]{:S(2)}, u32[]{:S(2)}) %collective-permute-start.5) | collective-permute-done | bytes 40992 | tf_op jit(solution)/shard_map/ppermute | solution.py:15
  136.8 16.2 %all-gather.5.cloned.1.call-done = bf16[3,3,3,256,256]{3,4,2,1,0:T(8,128)(2,1)} async-done(((bf16[3,3,3,256,8]{3,4,2,1,0:T(8,128)(2,1)}), bf16[3,3,3,256,256]{3,4,2,1,0:T(8,128)(2,1)}) %all-gather.5.cloned.1.call-update) | async-done | bytes 3538960 | tf_op jit(solution)/shard_map/all_gather | solution.py:91
  153.0 3.3 %fusion.40 = (bf16[1,3,3,256,256]{3,4,2,1,0:T(8,128)(2,1)S(1)}, bf16[1,3,3,256,256]{3,4,2,1,0:T(8,128)(2,1)S(1)}, bf16[1,3,3,256,256]{3,4,2,1,0:T(8,128)(2,1)}) fusion(bf16[3,3,3,256,256]{3,4,2,1,0:T(8,128)(2,1)} %all-gather.5.cloned.1.call-done), kind=kLoop, calls=%fused_computation.110 | loop fusion | bytes 7077888 | tf_op jit(solution)/shard_map/slice | solution.py:55
  156.3 2.4 %copy.49 = bf16[1,3,3,256,256]{4,3,2,1,0:T(8,128)(2,1)} copy(bf16[1,3,3,256,256]{3,4,2,1,0:T(8,128)(2,1)} %get-tuple-element.7) | data formatting | bytes 2359296
  158.7 1.6 copy.50
  161.0 2.4 %fusion.48 = f32[8,8,4,256]{3,2,1,0:T(4,128)S(1)} fusion(bf16[10,8,4,2304]{3,2,1,0:T(4,128)(2,1)} %slice_dynamic-update-slice_fusion.9, bf16[2304,256,1,1]{1,0,3,2:T(8,128)(2,1)} %bitcast.115), kind=kOutput, calls=%fused_computation.119 | convolution fusion | flops 301989888 | bytes 2916352 | tf_op jit(solution)/shard_map/dot_general | solution.py:51
  163.4 2.0 convolution_add_fusion.3
  165.4 2.1 %fusion.14 = bf16[8,8,4,256]{3,2,1,0:T(4,128)(2,1)S(1)} fusion(f32[8,8,4,256]{3,2,1,0:T(4,128)S(1)} %convert_element_type.86, f32[8,8,4,256]{3,2,1,0:T(4,128)S(1)} %convolution_add_fusion.3, bf16[10,8,4,2304]{3,2,1,0:T(4,128)(2,1)} %slice_dynamic-update-slice_fusion.9, bf16[2304,256,1,1]{1,0,3,2:T(8,128)(2,1)S(1)} %bitcast.114), kind=kOutput, calls=%fused_computation.21 | convolution fusion | flops 302186496 | bytes 3309568 | tf_op jit(solution)/shard_map/dot_general | solution.py:53
  168.2 2.7 %collective-permute-start.6 = (bf16[8,1,8,128]{3,2,1,0:T(8,128)(2,1)S(1)}, bf16[8,1,8,128]{3,2,1,0:T(8,128)(2,1)S(1)}, u32[]{:S(2)}, u32[]{:S(2)}) collective-permute-start(bf16[8,1,8,128]{3,2,1,0:T(8,128)(2,1)S(1)} %get-tuple-element.18), channel_id=1, source_target_pairs={{0,32},{32,64},{64,96},{96,128},{128,160},{160,192},{192,224},{224... | collective-permute-start | bytes 49160 | tf_op jit(solution)/shard_map/ppermute | solution.py:14
  170.9 2.6 %collective-permute-start.7 = (bf16[8,1,8,128]{3,2,1,0:T(8,128)(2,1)S(1)}, bf16[8,1,8,128]{3,2,1,0:T(8,128)(2,1)S(1)}, u32[]{:S(2)}, u32[]{:S(2)}) collective-permute-start(bf16[8,1,8,128]{3,2,1,0:T(8,128)(2,1)S(1)} %get-tuple-element.19), channel_id=1, source_target_pairs={{32,0},{64,32},{96,64},{128,96},{160,128},{192,160},{224,192},{256... | collective-permute-start | bytes 49160 | tf_op jit(solution)/shard_map/ppermute | solution.py:15
  173.5 4.0 %collective-permute-done.7 = bf16[8,1,8,128]{3,2,1,0:T(8,128)(2,1)S(1)} collective-permute-done((bf16[8,1,8,128]{3,2,1,0:T(8,128)(2,1)S(1)}, bf16[8,1,8,128]{3,2,1,0:T(8,128)(2,1)S(1)}, u32[]{:S(2)}, u32[]{:S(2)}) %collective-permute-start.7) | collective-permute-done | bytes 16416 | tf_op jit(solution)/shard_map/ppermute | solution.py:15
  177.6 5.2 %collective-permute-start.8 = (bf16[8,18,1,128]{3,2,1,0:T(2,128)(2,1)S(1)}, bf16[8,18,1,128]{3,2,1,0:T(2,128)(2,1)S(1)}, u32[]{:S(2)}, u32[]{:S(2)}) collective-permute-start(bf16[8,18,1,128]{3,2,1,0:T(2,128)(2,1)S(1)} %get-tuple-element.16), channel_id=1, source_target_pairs={{0,1},{1,2},{2,3},{3,4},{4,5},{5,6},{6,7},{7,8},{8,9},{9,10},{10,1... | collective-permute-start | bytes 110600 | tf_op jit(solution)/shard_map/ppermute | solution.py:14
  182.9 1.9 collective-permute-start.9
  184.9 3.6 %collective-permute-done.9 = bf16[8,18,1,128]{3,2,1,0:T(2,128)(2,1)S(1)} collective-permute-done((bf16[8,18,1,128]{3,2,1,0:T(2,128)(2,1)S(1)}, bf16[8,18,1,128]{3,2,1,0:T(2,128)(2,1)S(1)}, u32[]{:S(2)}, u32[]{:S(2)}) %collective-permute-start.9) | collective-permute-done | bytes 36896 | tf_op jit(solution)/shard_map/ppermute | solution.py:15
  192.0 1.5 fusion.12
  (81 shorter events, 17.8 us)
Async XLA Ops:
  6.5 100.8 %copy-start = (bf16[512,256]{1,0:T(8,128)(2,1)S(1)}, bf16[512,256]{1,0:T(8,128)(2,1)}, u32[]{:S(2)}) copy-start(bf16[512,256]{1,0:T(8,128)(2,1)} %param.10) | copy-start | bytes 786436
  6.5 73.4 %copy-start.2 = (bf16[3,3,3,512,32]{3,4,2,1,0:T(8,128)(2,1)S(1)}, bf16[3,3,3,512,32]{3,4,2,1,0:T(8,128)(2,1)}, u32[]{:S(2)}) copy-start(bf16[3,3,3,512,32]{3,4,2,1,0:T(8,128)(2,1)} %param.7) | copy-start | bytes 2654212
  6.5 64.5 %all-gather.3.cloned.1.call-start = ((), (), s32[]{:S(2)}) async-start(), calls=%async_computation.1 | async-start | bytes 1114112 | tf_op jit(solution)/shard_map/all_gather | solution.py:96
  9.2 143.8 %all-gather.5.cloned.1.call-start = ((), (), s32[]{:S(2)}) async-start(), calls=%async_computation.2 | async-start | bytes 3649536 | tf_op jit(solution)/shard_map/all_gather | solution.py:91
  73.0 11.2 %collective-permute-start = (bf16[8,64,1,512]{3,1,2,0:T(8,128)(2,1)S(1)}, bf16[8,64,1,512]{3,1,2,0:T(8,128)(2,1)S(1)}, u32[]{:S(2)}, u32[]{:S(2)}) collective-permute-start(bf16[8,64,1,512]{3,1,2,0:T(8,128)(2,1)S(1)} %get-tuple-element.8), channel_id=1, source_target_pairs={{0,1},{1,2},{2,3},{3,4},{4,5},{5,6},{6,7},{7,8},{8,9},{9,10},{10,1... | collective-permute-start | bytes 1572872 | tf_op jit(solution)/shard_map/ppermute | solution.py:14
  78.0 10.5 %collective-permute-start.1 = (bf16[8,64,1,512]{3,1,2,0:T(8,128)(2,1)S(1)}, bf16[8,64,1,512]{3,1,2,0:T(8,128)(2,1)S(1)}, u32[]{:S(2)}, u32[]{:S(2)}) collective-permute-start(bf16[8,64,1,512]{3,1,2,0:T(8,128)(2,1)S(1)} %get-tuple-element.9), channel_id=1, source_target_pairs={{1,0},{2,1},{3,2},{4,3},{5,4},{6,5},{7,6},{8,7},{9,8},{10,9},{11,1... | collective-permute-start | bytes 1572872 | tf_op jit(solution)/shard_map/ppermute | solution.py:15
  96.4 10.9 %copy-start.4 = (bf16[8,4,2,512]{3,2,1,0:T(2,128)(2,1)S(1)}, bf16[8,4,2,512]{3,2,1,0:T(2,128)(2,1)}, u32[]{:S(2)}) copy-start(bf16[8,4,2,512]{3,2,1,0:T(2,128)(2,1)} %param.6) | copy-start | bytes 196612
  108.0 5.6 %collective-permute-start.2 = (bf16[8,1,4,256]{3,2,1,0:T(4,128)(2,1)S(1)}, bf16[8,1,4,256]{3,2,1,0:T(4,128)(2,1)S(1)}, u32[]{:S(2)}, u32[]{:S(2)}) collective-permute-start(bf16[8,1,4,256]{3,2,1,0:T(4,128)(2,1)S(1)} %get-tuple-element.23), channel_id=1, source_target_pairs={{0,32},{32,64},{64,96},{96,128},{128,160},{160,192},{192,224},{224... | collective-permute-start | bytes 49160 | tf_op jit(solution)/shard_map/ppermute | solution.py:14
  111.7 6.6 %collective-permute-start.3 = (bf16[8,1,4,256]{3,2,1,0:T(4,128)(2,1)S(1)}, bf16[8,1,4,256]{3,2,1,0:T(4,128)(2,1)S(1)}, u32[]{:S(2)}, u32[]{:S(2)}) collective-permute-start(bf16[8,1,4,256]{3,2,1,0:T(4,128)(2,1)S(1)} %get-tuple-element.22), channel_id=1, source_target_pairs={{32,0},{64,32},{96,64},{128,96},{160,128},{192,160},{224,192},{256... | collective-permute-start | bytes 49160 | tf_op jit(solution)/shard_map/ppermute | solution.py:15
  118.4 7.2 %collective-permute-start.4 = (bf16[8,10,1,256]{3,2,1,0:T(2,128)(2,1)S(1)}, bf16[8,10,1,256]{3,2,1,0:T(2,128)(2,1)S(1)}, u32[]{:S(2)}, u32[]{:S(2)}) collective-permute-start(bf16[8,10,1,256]{3,2,1,0:T(2,128)(2,1)S(1)} %get-tuple-element.20), channel_id=1, source_target_pairs={{0,1},{1,2},{2,3},{3,4},{4,5},{5,6},{6,7},{7,8},{8,9},{9,10},{10,1... | collective-permute-start | bytes 122888 | tf_op jit(solution)/shard_map/ppermute | solution.py:14
  123.1 6.3 %collective-permute-start.5 = (bf16[8,10,1,256]{3,2,1,0:T(2,128)(2,1)S(1)}, bf16[8,10,1,256]{3,2,1,0:T(2,128)(2,1)S(1)}, u32[]{:S(2)}, u32[]{:S(2)}) collective-permute-start(bf16[8,10,1,256]{3,2,1,0:T(2,128)(2,1)S(1)} %get-tuple-element.21), channel_id=1, source_target_pairs={{1,0},{2,1},{3,2},{4,3},{5,4},{6,5},{7,6},{8,7},{9,8},{10,9},{11,1... | collective-permute-start | bytes 122888 | tf_op jit(solution)/shard_map/ppermute | solution.py:15
  161.0 2.4 %copy-start.1 = (bf16[1,3,3,256,256]{4,3,2,1,0:T(8,128)(2,1)S(1)}, bf16[1,3,3,256,256]{4,3,2,1,0:T(8,128)(2,1)}, u32[]{:S(2)}) copy-start(bf16[1,3,3,256,256]{4,3,2,1,0:T(8,128)(2,1)} %copy.50) | copy-start | bytes 3538948
  165.4 2.1 %copy-start.5 = (bf16[256,128]{1,0:T(8,128)(2,1)S(1)}, bf16[256,128]{1,0:T(8,128)(2,1)}, u32[]{:S(2)}) copy-start(bf16[256,128]{1,0:T(8,128)(2,1)} %param.11) | copy-start | bytes 196612
  165.4 19.4 %copy-start.3 = (bf16[3,3,3,128,128]{4,3,2,1,0:T(8,128)(2,1)S(1)}, bf16[3,3,3,128,128]{4,3,2,1,0:T(8,128)(2,1)}, u32[]{:S(2)}) copy-start(bf16[3,3,3,128,128]{4,3,2,1,0:T(8,128)(2,1)} %param.9) | copy-start | bytes 2654212
  168.2 5.3 %collective-permute-start.6 = (bf16[8,1,8,128]{3,2,1,0:T(8,128)(2,1)S(1)}, bf16[8,1,8,128]{3,2,1,0:T(8,128)(2,1)S(1)}, u32[]{:S(2)}, u32[]{:S(2)}) collective-permute-start(bf16[8,1,8,128]{3,2,1,0:T(8,128)(2,1)S(1)} %get-tuple-element.18), channel_id=1, source_target_pairs={{0,32},{32,64},{64,96},{96,128},{128,160},{160,192},{192,224},{224... | collective-permute-start | bytes 49160 | tf_op jit(solution)/shard_map/ppermute | solution.py:14
  170.9 6.6 %collective-permute-start.7 = (bf16[8,1,8,128]{3,2,1,0:T(8,128)(2,1)S(1)}, bf16[8,1,8,128]{3,2,1,0:T(8,128)(2,1)S(1)}, u32[]{:S(2)}, u32[]{:S(2)}) collective-permute-start(bf16[8,1,8,128]{3,2,1,0:T(8,128)(2,1)S(1)} %get-tuple-element.19), channel_id=1, source_target_pairs={{32,0},{64,32},{96,64},{128,96},{160,128},{192,160},{224,192},{256... | collective-permute-start | bytes 49160 | tf_op jit(solution)/shard_map/ppermute | solution.py:15
  177.6 7.3 %collective-permute-start.8 = (bf16[8,18,1,128]{3,2,1,0:T(2,128)(2,1)S(1)}, bf16[8,18,1,128]{3,2,1,0:T(2,128)(2,1)S(1)}, u32[]{:S(2)}, u32[]{:S(2)}) collective-permute-start(bf16[8,18,1,128]{3,2,1,0:T(2,128)(2,1)S(1)} %get-tuple-element.16), channel_id=1, source_target_pairs={{0,1},{1,2},{2,3},{3,4},{4,5},{5,6},{6,7},{7,8},{8,9},{9,10},{10,1... | collective-permute-start | bytes 110600 | tf_op jit(solution)/shard_map/ppermute | solution.py:14
  182.9 5.7 %collective-permute-start.9 = (bf16[8,18,1,128]{3,2,1,0:T(2,128)(2,1)S(1)}, bf16[8,18,1,128]{3,2,1,0:T(2,128)(2,1)S(1)}, u32[]{:S(2)}, u32[]{:S(2)}) collective-permute-start(bf16[8,18,1,128]{3,2,1,0:T(2,128)(2,1)S(1)} %get-tuple-element.17), channel_id=1, source_target_pairs={{1,0},{2,1},{3,2},{4,3},{5,4},{6,5},{7,6},{8,7},{9,8},{10,9},{11,1... | collective-permute-start | bytes 110600 | tf_op jit(solution)/shard_map/ppermute | solution.py:15
Sparse Core Ops, SparseCore 0:
  10.4 60.6 all-gather.2
  73.1 79.7 all-gather.4
where the time goes:
time: 201 us; the launch traced here: 200 us
  waiting for transfers between devices  102 us (51%)
  starting transfers between devices  31.8 us (16%)
  local copies, waits for them, and re-layouts  20.9 us (10%)
  matrix products  14.4 us (7%)
  between operations  13.9 us (7%)
  blocking collectives  9.77 us (5%)
  other arithmetic  7.18 us (4%)
    all_gather x1, waiting for transfers between devices, body(): whole = lax.all_gather(first_act, 'grp', axis=1, tiled=True)  61.1 us
    ppermute x5, starting transfers between devices, with_halo(): before = lax.ppermute(last, axis, up)  21.3 us
    ppermute x5, waiting for transfers between devices, with_halo(): after = lax.ppermute(initial, axis, down)  20.3 us
    all_gather x1, waiting for transfers between devices, middle_conv(): lax.all_gather(mid_filters, 'tile', axis=4, tiled=True)  16.2 us
    unnamed x35, local copies, waits for them, and re-layouts  12.7 us
    ppermute x5, starting transfers between devices, with_halo(): after = lax.ppermute(initial, axis, down)  10.5 us
    all_to_all x1, blocking collectives, body(): lax.all_to_all(filtered, 'grp', split_axis=1, concat_axis=3, tiled=True)  9.77 us
    dot_general x4, matrix products, apply_columns(): jnp.dot(columns[frame_step:frame_step + frames], folded[frame_step], pref...  6.33 us
  transfers between devices with their start and end apart: 12, of which 8 were waited for; matrix products, arithmetic and copies ran while one was open for 10% of the time, Pallas kernels for 0%

commit v1 on v0

--- a/solution.py
+++ b/solution.py
@@ -88,7 +88,12 @@
 
 def middle_conv(extended, mid_filters):
     columns = stencil_columns(extended)
-    return apply_columns(columns, lax.all_gather(mid_filters, "tile", axis=4, tiled=True))
+    return apply_columns(
+        columns,
+        jnp.concatenate(
+            lax.all_to_all(jnp.stack([mid_filters] * lax.axis_size("tile")), "tile", 0, 0), axis=4
+        ),
+    )
 
 
 def body(latent, coarse_filters, mid_filters, fine_filters, coarse_proj, mid_proj):

time: 201 us -> 323 us (1.61)
  waiting for transfers between devices: 102 us -> 220 us
  starting transfers between devices: 31.8 us -> 50.6 us
  local copies, waits for them, and re-layouts: 20.9 us -> 11 us
  matrix products: 14.4 us -> 10.2 us
    ppermute x5, waiting for transfers between devices: 4.11 us -> 132 us  [with_halo(): before = lax.ppermute(last, axis, up)]
    all_gather x1 -> x0, waiting for transfers between devices: 16.2 us -> none  [middle_conv(): lax.all_gather(mid_filters, 'tile', axis=4, tiled=True)]
    all_to_all x0 -> x1, starting transfers between devices: none -> 13.8 us  [middle_conv(): lax.all_to_all(jnp.stack([mid_filters] * lax.axis_size('tile')), 'tile',...]
    unnamed x35 -> x32, local copies, waits for them, and re-layouts: 12.7 us -> 2.52 us
    ppermute x5, starting transfers between devices: 21.3 us -> 27 us  [with_halo(): before = lax.ppermute(last, axis, up)]
    ppermute x5, waiting for transfers between devices: 20.3 us -> 25.3 us  [with_halo(): after = lax.ppermute(initial, axis, down)]
  transfers between devices with their start and end apart: 12 -> 12, of which waited for: 8 -> 9; matrix products, arithmetic and copies ran while one was open for 10% -> 1% of each run, Pallas kernels for 0% -> 0%
where the time goes in v1:
time: 323 us
  waiting for transfers between devices  220 us (68%)
  starting transfers between devices  50.6 us (16%)
  between operations  13.9 us (4%)
  local copies, waits for them, and re-layouts  11 us (3%)
  matrix products  10.2 us (3%)
  blocking collectives  9.77 us (3%)
  other arithmetic  7.17 us (2%)
    ppermute x5, waiting for transfers between devices, with_halo(): before = lax.ppermute(last, axis, up)  132 us
    all_gather x1, waiting for transfers between devices, body(): whole = lax.all_gather(first_act, 'grp', axis=1, tiled=True)  61.9 us
    ppermute x5, starting transfers between devices, with_halo(): before = lax.ppermute(last, axis, up)  27 us
    ppermute x5, waiting for transfers between devices, with_halo(): after = lax.ppermute(initial, axis, down)  25.3 us
    all_to_all x1, starting transfers between devices, middle_conv(): lax.all_to_all(jnp.stack([mid_filters] * lax.axis_size('tile')), 'tile',...  13.8 us
    ppermute x5, starting transfers between devices, with_halo(): after = lax.ppermute(initial, axis, down)  9.78 us
    all_to_all x1, blocking collectives, body(): lax.all_to_all(filtered, 'grp', split_axis=1, concat_axis=3, tiled=True)  9.77 us
  transfers between devices with their start and end apart: 12, of which 9 were waited for; matrix products, arithmetic and copies ran while one was open for 1% of the time, Pallas kernels for 0%

profile of v1, /device:TPU:7, one launch (start us, length us, event | category | flops | bytes accessed | tf_op | source)
XLA Modules:
  0.0 322.7 jit_solution(10591971579450849039)
XLA Ops:
  6.5 1.0 fusion.34
  7.6 1.6 fusion.33
  9.2 61.9 %all-gather.2.cloned.1.call-done = bf16[8,64,2,512]{3,0,2,1:T(8,128)(2,1)} async-done(((bf16[8,4,2,512]{3,0,2,1:T(8,128)(2,1)}), bf16[8,64,2,512]{3,0,2,1:T(8,128)(2,1)}) %all-gather.2.cloned.1.call-update) | async-done | bytes 1048592 | tf_op jit(solution)/shard_map/all_gather | solution.py:101
  71.1 1.8 copy.26
  73.0 5.1 %collective-permute-start = (bf16[8,64,1,512]{3,1,2,0:T(8,128)(2,1)S(1)}, bf16[8,64,1,512]{3,1,2,0:T(8,128)(2,1)S(1)}, u32[]{:S(2)}, u32[]{:S(2)}) collective-permute-start(bf16[8,64,1,512]{3,1,2,0:T(8,128)(2,1)S(1)} %get-tuple-element.8), channel_id=1, source_target_pairs={{0,1},{1,2},{2,3},{3,4},{4,5},{5,6},{6,7},{7,8},{8,9},{9,10},{10,1... | collective-permute-start | bytes 1572872 | tf_op jit(solution)/shard_map/ppermute | solution.py:14
  78.0 1.9 collective-permute-start.1
  80.0 4.1 %collective-permute-done = bf16[8,64,1,512]{3,1,2,0:T(8,128)(2,1)S(1)} collective-permute-done((bf16[8,64,1,512]{3,1,2,0:T(8,128)(2,1)S(1)}, bf16[8,64,1,512]{3,1,2,0:T(8,128)(2,1)S(1)}, u32[]{:S(2)}, u32[]{:S(2)}) %collective-permute-start) | collective-permute-done | bytes 524320 | tf_op jit(solution)/shard_map/ppermute | solution.py:14
  84.1 4.4 %collective-permute-done.1 = bf16[8,64,1,512]{3,1,2,0:T(8,128)(2,1)S(1)} collective-permute-done((bf16[8,64,1,512]{3,1,2,0:T(8,128)(2,1)S(1)}, bf16[8,64,1,512]{3,1,2,0:T(8,128)(2,1)S(1)}, u32[]{:S(2)}, u32[]{:S(2)}) %collective-permute-start.1) | collective-permute-done | bytes 524320 | tf_op jit(solution)/shard_map/ppermute | solution.py:15
  88.5 1.0 fusion.5
  89.6 1.4 fusion.47
  91.0 1.4 fusion.50
  92.5 1.4 fusion.51
  93.9 2.5 fusion.24
  97.0 9.8 %all_to_all.14 = bf16[16,2,1024]{2,1,0:T(2,128)(2,1)S(1)} all-to-all(bf16[16,2,1024]{2,1,0:T(2,128)(2,1)S(1)} %reshape.96), channel_id=1, replica_groups=mesh['grp'=16,'tile'=32] {'grp'}, dimensions={0} | all-to-all | bytes 131072 | tf_op jit(solution)/shard_map/all_to_all | solution.py:105
  106.8 2.0 stack.2
  108.8 13.8 %all-to-all-start.1 = ((bf16[32,3,3,3,256,8]{4,5,3,2,1,0:T(8,128)(2,1)}), bf16[32,3,3,3,256,8]{4,5,3,2,1,0:T(8,128)(2,1)}, u32[]{:S(2)}, u32[]{:S(2)}) async-start(bf16[32,3,3,3,256,8]{4,5,3,2,1,0:T(8,128)(2,1)} %stack.2), calls=%async_computation.1 | async-start | bytes 7077888 | tf_op jit(solution)/shard_map/all_to_all | solution.py:94
  123.9 3.7 %collective-permute-start.2 = (bf16[8,1,4,256]{3,2,1,0:T(4,128)(2,1)S(1)}, bf16[8,1,4,256]{3,2,1,0:T(4,128)(2,1)S(1)}, u32[]{:S(2)}, u32[]{:S(2)}) collective-permute-start(bf16[8,1,4,256]{3,2,1,0:T(4,128)(2,1)S(1)} %get-tuple-element.23), channel_id=1, source_target_pairs={{0,32},{32,64},{64,96},{96,128},{128,160},{160,192},{192,224},{224... | collective-permute-start | bytes 49160 | tf_op jit(solution)/shard_map/ppermute | solution.py:14
  127.5 1.9 collective-permute-start.3
  129.6 5.0 %collective-permute-done.3 = bf16[8,1,4,256]{3,2,1,0:T(4,128)(2,1)S(1)} collective-permute-done((bf16[8,1,4,256]{3,2,1,0:T(4,128)(2,1)S(1)}, bf16[8,1,4,256]{3,2,1,0:T(4,128)(2,1)S(1)}, u32[]{:S(2)}, u32[]{:S(2)}) %collective-permute-start.3) | collective-permute-done | bytes 16416 | tf_op jit(solution)/shard_map/ppermute | solution.py:15
  134.7 4.6 %collective-permute-start.4 = (bf16[8,10,1,256]{3,2,1,0:T(2,128)(2,1)S(1)}, bf16[8,10,1,256]{3,2,1,0:T(2,128)(2,1)S(1)}, u32[]{:S(2)}, u32[]{:S(2)}) collective-permute-start(bf16[8,10,1,256]{3,2,1,0:T(2,128)(2,1)S(1)} %get-tuple-element.20), channel_id=1, source_target_pairs={{0,1},{1,2},{2,3},{3,4},{4,5},{5,6},{6,7},{7,8},{8,9},{9,10},{10,1... | collective-permute-start | bytes 122888 | tf_op jit(solution)/shard_map/ppermute | solution.py:14
  139.3 2.1 collective-permute-start.5
  141.8 127.7 %collective-permute-done.4 = bf16[8,10,1,256]{3,2,1,0:T(2,128)(2,1)S(1)} collective-permute-done((bf16[8,10,1,256]{3,2,1,0:T(2,128)(2,1)S(1)}, bf16[8,10,1,256]{3,2,1,0:T(2,128)(2,1)S(1)}, u32[]{:S(2)}, u32[]{:S(2)}) %collective-permute-start.4) | collective-permute-done | bytes 40992 | tf_op jit(solution)/shard_map/ppermute | solution.py:14
  269.5 7.7 %collective-permute-done.5 = bf16[8,10,1,256]{3,2,1,0:T(2,128)(2,1)S(1)} collective-permute-done((bf16[8,10,1,256]{3,2,1,0:T(2,128)(2,1)S(1)}, bf16[8,10,1,256]{3,2,1,0:T(2,128)(2,1)S(1)}, u32[]{:S(2)}, u32[]{:S(2)}) %collective-permute-start.5) | collective-permute-done | bytes 40992 | tf_op jit(solution)/shard_map/ppermute | solution.py:15
  278.5 1.0 all-to-all-done.1
  279.5 2.2 fusion.40
  284.8 3.7 %collective-permute-start.6 = (bf16[8,1,8,128]{3,2,1,0:T(8,128)(2,1)S(1)}, bf16[8,1,8,128]{3,2,1,0:T(8,128)(2,1)S(1)}, u32[]{:S(2)}, u32[]{:S(2)}) collective-permute-start(bf16[8,1,8,128]{3,2,1,0:T(8,128)(2,1)S(1)} %get-tuple-element.18), channel_id=1, source_target_pairs={{0,32},{32,64},{64,96},{96,128},{128,160},{160,192},{192,224},{224... | collective-permute-start | bytes 49160 | tf_op jit(solution)/shard_map/ppermute | solution.py:14
  288.5 1.9 collective-permute-start.7
  290.4 4.7 %collective-permute-done.7 = bf16[8,1,8,128]{3,2,1,0:T(8,128)(2,1)S(1)} collective-permute-done((bf16[8,1,8,128]{3,2,1,0:T(8,128)(2,1)S(1)}, bf16[8,1,8,128]{3,2,1,0:T(8,128)(2,1)S(1)}, u32[]{:S(2)}, u32[]{:S(2)}) %collective-permute-start.7) | collective-permute-done | bytes 16416 | tf_op jit(solution)/shard_map/ppermute | solution.py:15
  295.2 10.0 %collective-permute-start.8 = (bf16[8,18,1,128]{3,2,1,0:T(2,128)(2,1)S(1)}, bf16[8,18,1,128]{3,2,1,0:T(2,128)(2,1)S(1)}, u32[]{:S(2)}, u32[]{:S(2)}) collective-permute-start(bf16[8,18,1,128]{3,2,1,0:T(2,128)(2,1)S(1)} %get-tuple-element.16), channel_id=1, source_target_pairs={{0,1},{1,2},{2,3},{3,4},{4,5},{5,6},{6,7},{7,8},{8,9},{9,10},{10,1... | collective-permute-start | bytes 110600 | tf_op jit(solution)/shard_map/ppermute | solution.py:14
  305.2 1.9 collective-permute-start.9
  307.3 3.6 %collective-permute-done.9 = bf16[8,18,1,128]{3,2,1,0:T(2,128)(2,1)S(1)} collective-permute-done((bf16[8,18,1,128]{3,2,1,0:T(2,128)(2,1)S(1)}, bf16[8,18,1,128]{3,2,1,0:T(2,128)(2,1)S(1)}, u32[]{:S(2)}, u32[]{:S(2)}) %collective-permute-start.9) | collective-permute-done | bytes 36896 | tf_op jit(solution)/shard_map/ppermute | solution.py:15
  314.4 1.5 fusion.12
  (78 shorter events, 10.4 us)
Async XLA Ops:
  6.5 116.7 %copy-start = (bf16[512,256]{1,0:T(8,128)(2,1)S(1)}, bf16[512,256]{1,0:T(8,128)(2,1)}, u32[]{:S(2)}) copy-start(bf16[512,256]{1,0:T(8,128)(2,1)} %param.10) | copy-start | bytes 786436
  6.5 73.4 %copy-start.1 = (bf16[3,3,3,512,32]{3,4,2,1,0:T(8,128)(2,1)S(1)}, bf16[3,3,3,512,32]{3,4,2,1,0:T(8,128)(2,1)}, u32[]{:S(2)}) copy-start(bf16[3,3,3,512,32]{3,4,2,1,0:T(8,128)(2,1)} %param.7) | copy-start | bytes 2654212
  6.5 64.5 %all-gather.2.cloned.1.call-start = ((), (), s32[]{:S(2)}) async-start(), calls=%async_computation.2 | async-start | bytes 1114112 | tf_op jit(solution)/shard_map/all_gather | solution.py:101
  73.0 11.2 %collective-permute-start = (bf16[8,64,1,512]{3,1,2,0:T(8,128)(2,1)S(1)}, bf16[8,64,1,512]{3,1,2,0:T(8,128)(2,1)S(1)}, u32[]{:S(2)}, u32[]{:S(2)}) collective-permute-start(bf16[8,64,1,512]{3,1,2,0:T(8,128)(2,1)S(1)} %get-tuple-element.8), channel_id=1, source_target_pairs={{0,1},{1,2},{2,3},{3,4},{4,5},{5,6},{6,7},{7,8},{8,9},{9,10},{10,1... | collective-permute-start | bytes 1572872 | tf_op jit(solution)/shard_map/ppermute | solution.py:14
  78.0 10.5 %collective-permute-start.1 = (bf16[8,64,1,512]{3,1,2,0:T(8,128)(2,1)S(1)}, bf16[8,64,1,512]{3,1,2,0:T(8,128)(2,1)S(1)}, u32[]{:S(2)}, u32[]{:S(2)}) collective-permute-start(bf16[8,64,1,512]{3,1,2,0:T(8,128)(2,1)S(1)} %get-tuple-element.9), channel_id=1, source_target_pairs={{1,0},{2,1},{3,2},{4,3},{5,4},{6,5},{7,6},{8,7},{9,8},{10,9},{11,1... | collective-permute-start | bytes 1572872 | tf_op jit(solution)/shard_map/ppermute | solution.py:15
  93.9 12.8 %copy-start.4 = (bf16[3,3,3,256,8]{3,4,2,1,0:T(8,128)(2,1)S(1)}, bf16[3,3,3,256,8]{3,4,2,1,0:T(8,128)(2,1)}, u32[]{:S(2)}) copy-start(bf16[3,3,3,256,8]{3,4,2,1,0:T(8,128)(2,1)} %param.8) | copy-start | bytes 331780
  108.8 14.4 %copy-start.3 = (bf16[8,4,2,512]{3,2,1,0:T(2,128)(2,1)S(1)}, bf16[8,4,2,512]{3,2,1,0:T(2,128)(2,1)}, u32[]{:S(2)}) copy-start(bf16[8,4,2,512]{3,2,1,0:T(2,128)(2,1)} %param.6) | copy-start | bytes 196612
  108.8 170.7 %all-to-all-start.1 = ((bf16[32,3,3,3,256,8]{4,5,3,2,1,0:T(8,128)(2,1)}), bf16[32,3,3,3,256,8]{4,5,3,2,1,0:T(8,128)(2,1)}, u32[]{:S(2)}, u32[]{:S(2)}) async-start(bf16[32,3,3,3,256,8]{4,5,3,2,1,0:T(8,128)(2,1)} %stack.2), calls=%async_computation.1 | async-start | bytes 7077888 | tf_op jit(solution)/shard_map/all_to_all | solution.py:94
  123.9 5.6 %collective-permute-start.2 = (bf16[8,1,4,256]{3,2,1,0:T(4,128)(2,1)S(1)}, bf16[8,1,4,256]{3,2,1,0:T(4,128)(2,1)S(1)}, u32[]{:S(2)}, u32[]{:S(2)}) collective-permute-start(bf16[8,1,4,256]{3,2,1,0:T(4,128)(2,1)S(1)} %get-tuple-element.23), channel_id=1, source_target_pairs={{0,32},{32,64},{64,96},{96,128},{128,160},{160,192},{192,224},{224... | collective-permute-start | bytes 49160 | tf_op jit(solution)/shard_map/ppermute | solution.py:14
  127.5 7.0 %collective-permute-start.3 = (bf16[8,1,4,256]{3,2,1,0:T(4,128)(2,1)S(1)}, bf16[8,1,4,256]{3,2,1,0:T(4,128)(2,1)S(1)}, u32[]{:S(2)}, u32[]{:S(2)}) collective-permute-start(bf16[8,1,4,256]{3,2,1,0:T(4,128)(2,1)S(1)} %get-tuple-element.22), channel_id=1, source_target_pairs={{32,0},{64,32},{96,64},{128,96},{160,128},{192,160},{224,192},{256... | collective-permute-start | bytes 49160 | tf_op jit(solution)/shard_map/ppermute | solution.py:15
  134.7 134.8 %collective-permute-start.4 = (bf16[8,10,1,256]{3,2,1,0:T(2,128)(2,1)S(1)}, bf16[8,10,1,256]{3,2,1,0:T(2,128)(2,1)S(1)}, u32[]{:S(2)}, u32[]{:S(2)}) collective-permute-start(bf16[8,10,1,256]{3,2,1,0:T(2,128)(2,1)S(1)} %get-tuple-element.20), channel_id=1, source_target_pairs={{0,1},{1,2},{2,3},{3,4},{4,5},{5,6},{6,7},{7,8},{8,9},{9,10},{10,1... | collective-permute-start | bytes 122888 | tf_op jit(solution)/shard_map/ppermute | solution.py:14
  139.3 138.0 %collective-permute-start.5 = (bf16[8,10,1,256]{3,2,1,0:T(2,128)(2,1)S(1)}, bf16[8,10,1,256]{3,2,1,0:T(2,128)(2,1)S(1)}, u32[]{:S(2)}, u32[]{:S(2)}) collective-permute-start(bf16[8,10,1,256]{3,2,1,0:T(2,128)(2,1)S(1)} %get-tuple-element.21), channel_id=1, source_target_pairs={{1,0},{2,1},{3,2},{4,3},{5,4},{6,5},{7,6},{8,7},{9,8},{10,9},{11,1... | collective-permute-start | bytes 122888 | tf_op jit(solution)/shard_map/ppermute | solution.py:15
  283.2 0.8 copy-start.5
  284.1 23.1 %copy-start.2 = (bf16[3,3,3,128,128]{4,3,2,1,0:T(8,128)(2,1)S(1)}, bf16[3,3,3,128,128]{4,3,2,1,0:T(8,128)(2,1)}, u32[]{:S(2)}) copy-start(bf16[3,3,3,128,128]{4,3,2,1,0:T(8,128)(2,1)} %param.9) | copy-start | bytes 2654212
  284.8 5.6 %collective-permute-start.6 = (bf16[8,1,8,128]{3,2,1,0:T(8,128)(2,1)S(1)}, bf16[8,1,8,128]{3,2,1,0:T(8,128)(2,1)S(1)}, u32[]{:S(2)}, u32[]{:S(2)}) collective-permute-start(bf16[8,1,8,128]{3,2,1,0:T(8,128)(2,1)S(1)} %get-tuple-element.18), channel_id=1, source_target_pairs={{0,32},{32,64},{64,96},{96,128},{128,160},{160,192},{192,224},{224... | collective-permute-start | bytes 49160 | tf_op jit(solution)/shard_map/ppermute | solution.py:14
  288.5 6.6 %collective-permute-start.7 = (bf16[8,1,8,128]{3,2,1,0:T(8,128)(2,1)S(1)}, bf16[8,1,8,128]{3,2,1,0:T(8,128)(2,1)S(1)}, u32[]{:S(2)}, u32[]{:S(2)}) collective-permute-start(bf16[8,1,8,128]{3,2,1,0:T(8,128)(2,1)S(1)} %get-tuple-element.19), channel_id=1, source_target_pairs={{32,0},{64,32},{96,64},{128,96},{160,128},{192,160},{224,192},{256... | collective-permute-start | bytes 49160 | tf_op jit(solution)/shard_map/ppermute | solution.py:15
  295.2 12.1 %collective-permute-start.8 = (bf16[8,18,1,128]{3,2,1,0:T(2,128)(2,1)S(1)}, bf16[8,18,1,128]{3,2,1,0:T(2,128)(2,1)S(1)}, u32[]{:S(2)}, u32[]{:S(2)}) collective-permute-start(bf16[8,18,1,128]{3,2,1,0:T(2,128)(2,1)S(1)} %get-tuple-element.16), channel_id=1, source_target_pairs={{0,1},{1,2},{2,3},{3,4},{4,5},{5,6},{6,7},{7,8},{8,9},{9,10},{10,1... | collective-permute-start | bytes 110600 | tf_op jit(solution)/shard_map/ppermute | solution.py:14
  305.2 5.7 %collective-permute-start.9 = (bf16[8,18,1,128]{3,2,1,0:T(2,128)(2,1)S(1)}, bf16[8,18,1,128]{3,2,1,0:T(2,128)(2,1)S(1)}, u32[]{:S(2)}, u32[]{:S(2)}) collective-permute-start(bf16[8,18,1,128]{3,2,1,0:T(2,128)(2,1)S(1)} %get-tuple-element.17), channel_id=1, source_target_pairs={{1,0},{2,1},{3,2},{4,3},{5,4},{6,5},{7,6},{8,7},{9,8},{10,9},{11,1... | collective-permute-start | bytes 110600 | tf_op jit(solution)/shard_map/ppermute | solution.py:15
Sparse Core Ops, SparseCore 0:
  10.4 60.6 all-gather.1
